TPU v7x, 256 devices: a whole 4x4x8 slice. The times are simulated.
256 devices in a mesh: tile: 32 (over z, x), zslab: 8 (over y, core).
Axes of the slice: x: 4, y: 4, z: 8, core: 2. Of those that a mesh axis runs over, the one named last changes fastest.
Arguments:
- band: bfloat16 [32, 4, 128, 64, 512], P('tile', None, 'zslab'), may hold values from -6 to 6
- pairs: int32 [64, 4], replicated, may hold values from 0 to 31, as said below
- extents: int32 [64, 2], replicated, may hold values from 32 to 512, as said below
Outputs:
- maps: float32 [64, 128, 32, 256], P('tile', 'zslab')
Inputs may be any that keep to these rules, and one draw needn't show every extreme that they name: `pairs`: every slot (tile, face) with tile < 32 and face < 4 is named by exactly one pair, and a pair names two different slots. `extents`: column 0 lies in 32 to 64, column 1 in 256 to 512; some pair has both at their most.
All inputs are finite; a program needn't handle non-finite values.
Results may differ from a plain program's by a relative error of at most 0.012.
The roundings to bfloat16 on the way count: a program that leaves them out, or rounds other values in their place, can miss the bound.
Values may be sent and summed in bfloat16 or wider, within the bound.
A program may use at most 64 MiB of HBM per device.

v0:
```python
import math
import jax
import jax.numpy as jnp
from jax import lax
from jax.sharding import PartitionSpec as P

GX = 32
GY = 256
GZ = 128
FACES = 4


def dft_tables(length):
    indices = jnp.arange(length, dtype=jnp.int32)
    modular = indices[:, None] * indices[None, :] % length
    angles = modular.astype(jnp.float32) * (2.0 * math.pi / length)
    factor = 1.0 / math.sqrt(length)
    return (
        (jnp.cos(angles) * factor).astype(jnp.bfloat16),
        (jnp.sin(angles) * factor).astype(jnp.bfloat16),
    )


def product(form, left, right):
    return jnp.einsum(form, left, right, preferred_element_type=jnp.float32)


def reduce_resolution(image_volume, crop_bounds):
    row_mask = (
        jnp.arange(image_volume.shape[2], dtype=jnp.int32)[None, :] < crop_bounds[:, 0:1]
    ).astype(jnp.bfloat16)
    col_mask = (
        jnp.arange(image_volume.shape[3], dtype=jnp.int32)[None, :] < crop_bounds[:, 1:2]
    ).astype(jnp.bfloat16)
    masked = image_volume * row_mask[:, None, :, None] * col_mask[:, None, None, :]
    raw_cols = jnp.arange(image_volume.shape[3], dtype=jnp.int32)
    pooled_cols = jnp.arange(GY, dtype=jnp.int32)
    pooling = jnp.where(raw_cols[:, None] // 2 == pooled_cols[None, :], 0.5, 0.0).astype(
        jnp.bfloat16
    )
    along_pooled = product("szxy,yk->szxk", masked, pooling)
    shaped = along_pooled.reshape(image_volume.shape[0], image_volume.shape[1], GX, 2, GY)
    return (shaped[:, :, :, 0, :] + shaped[:, :, :, 1, :]).astype(jnp.bfloat16)


def cross_phase(owner_re, owner_im, pairs, tiles_here):
    first_dev = pairs[:, 0] // tiles_here
    first_pos = pairs[:, 0] % tiles_here * FACES + pairs[:, 1]
    second_tile_device = pairs[:, 2] // tiles_here
    second_pos = pairs[:, 2] % tiles_here * FACES + pairs[:, 3]
    first_re = owner_re[first_dev, :, first_pos].astype(jnp.float32)
    first_im = owner_im[first_dev, :, first_pos].astype(jnp.float32)
    second_re = owner_re[second_tile_device, :, second_pos].astype(jnp.float32)
    second_im = owner_im[second_tile_device, :, second_pos].astype(jnp.float32)
    cross_re = first_re * second_re + first_im * second_im
    cross_im = first_im * second_re - first_re * second_im
    scaled = jnp.sqrt(cross_re * cross_re + cross_im * cross_im + 1.0)
    return ((cross_re / scaled).astype(jnp.bfloat16), (cross_im / scaled).astype(jnp.bfloat16))


def inverse_z(phase_real_part, phase_im, tables_z):
    w_re = (
        product("pmjk,mz->pzjk", phase_real_part, tables_z[0])
        - product("pmjk,mz->pzjk", phase_im, tables_z[1])
    ).astype(jnp.bfloat16)
    w_im = (
        product("pmjk,mz->pzjk", phase_im, tables_z[0])
        + product("pmjk,mz->pzjk", phase_real_part, tables_z[1])
    ).astype(jnp.bfloat16)
    return (w_re, w_im)


def inverse_x(w_re, w_im, tables_x):
    v_re = (
        product("pzjk,jx->pzxk", w_re, tables_x[0]) - product("pzjk,jx->pzxk", w_im, tables_x[1])
    ).astype(jnp.bfloat16)
    v_im = (
        product("pzjk,jx->pzxk", w_im, tables_x[0]) + product("pzjk,jx->pzxk", w_re, tables_x[1])
    ).astype(jnp.bfloat16)
    return (v_re, v_im)


def shards(band, pairs, extents):
    tables_x = dft_tables(GX)
    tables_y = dft_tables(GY)
    tables_z = dft_tables(GZ)
    tiles_here = band.shape[0]
    slots = tiles_here * FACES
    zrows = band.shape[2]
    tile_pos = lax.axis_index("tile")
    global_slot = tile_pos * slots + jnp.arange(slots, dtype=jnp.int32)
    first_slot = pairs[:, 0] * FACES + pairs[:, 1]
    second_slot = pairs[:, 2] * FACES + pairs[:, 3]
    matches = (
        (first_slot[None, :] == global_slot[:, None])
        | (second_slot[None, :] == global_slot[:, None])
    ).astype(jnp.int32)
    crop_bounds = jnp.sum(matches[:, :, None] * extents[None, :, :], axis=1)
    image_volume = band.reshape(slots, zrows, 2 * GX, 2 * GY)
    reduced_volume = reduce_resolution(image_volume, crop_bounds)
    y_re = product("szxy,yk->szxk", reduced_volume, tables_y[0]).astype(jnp.bfloat16)
    y_im = (-product("szxy,yk->szxk", reduced_volume, tables_y[1])).astype(jnp.bfloat16)
    x_re = (
        product("szxk,xj->szjk", y_re, tables_x[0]) + product("szxk,xj->szjk", y_im, tables_x[1])
    ).astype(jnp.bfloat16)
    x_im = (
        product("szxk,xj->szjk", y_im, tables_x[0]) - product("szxk,xj->szjk", y_re, tables_x[1])
    ).astype(jnp.bfloat16)
    kx_part = GX // lax.axis_size("zslab")
    re_in = lax.all_to_all(x_re, "zslab", split_axis=2, concat_axis=1, tiled=True)
    im_in = lax.all_to_all(x_im, "zslab", split_axis=2, concat_axis=1, tiled=True)
    out_re = (
        product("szjk,zm->msjk", re_in, tables_z[0]) + product("szjk,zm->msjk", im_in, tables_z[1])
    ).astype(jnp.bfloat16)
    out_im = (
        product("szjk,zm->msjk", im_in, tables_z[0]) - product("szjk,zm->msjk", re_in, tables_z[1])
    ).astype(jnp.bfloat16)
    tile_count = lax.axis_size("tile")
    kz_part = GZ // tile_count
    spectra = (
        lax.all_to_all(out_re, "tile", split_axis=0, concat_axis=0, tiled=True),
        lax.all_to_all(out_im, "tile", split_axis=0, concat_axis=0, tiled=True),
    )
    owner_re = spectra[0].reshape(tile_count, kz_part, slots, kx_part, GY)
    owner_im = spectra[1].reshape(tile_count, kz_part, slots, kx_part, GY)
    phase_real_part, phase_im = cross_phase(owner_re, owner_im, pairs, tiles_here)
    returned = (
        lax.all_to_all(phase_real_part, "tile", split_axis=0, concat_axis=1, tiled=True),
        lax.all_to_all(phase_im, "tile", split_axis=0, concat_axis=1, tiled=True),
    )
    w_re, w_im = inverse_z(returned[0], returned[1], tables_z)
    v_re, v_im = inverse_x(
        lax.all_to_all(w_re, "zslab", split_axis=1, concat_axis=2, tiled=True),
        lax.all_to_all(w_im, "zslab", split_axis=1, concat_axis=2, tiled=True),
        tables_x,
    )
    return product("pzxk,ky->pzxy", v_re, tables_y[0]) - product("pzxk,ky->pzxy", v_im, tables_y[1])


def solution(mesh):
    placed = (P("tile", None, "zslab", None, None), P(), P())
    return jax.shard_map(
        shards,
        mesh=mesh,
        in_specs=placed,
        out_specs=P("tile", "zslab", None, None),
        check_vma=False,
    )
```

profile of v0, /device:TPU:1, one launch (start us, length us, event | category | flops | bytes accessed | tf_op | source)
XLA Modules:
  0.0 219.9 jit_solution(18191489263805402491)
XLA Ops:
  0.0 0.8 fusion.100
  0.9 0.1 or_convert_fusion
  0.9 0.8 multiply_reduce_fusion
  1.8 0.1 fusion.85
  1.8 7.2 %reshape.185 = bf16[4,16,32,2,512]{4,3,2,1,0:T(2,128)(2,1)} reshape(bf16[1,4,16,64,512]{4,3,2,1,0:T(8,128)(2,1)} %param.3) | data formatting | bytes 8388608 | tf_op jit(solution)/shard_map/reshape | solution.py:99
  9.1 0.1 compare_convert_fusion
  9.1 3.6 %fusion.1 = f32[4,16,32,2,256]{4,2,3,1,0:T(8,128)S(1)} fusion(bf16[4,16,32,2,512]{4,3,2,1,0:T(2,128)(2,1)} %reshape.185, bf16[4,512]{1,0:T(4,128)(2,1)S(1)} %fusion.85, bf16[4,32,2]{1,2,0:T(2,128)(2,1)S(1)} %compare_convert_fusion, s32[512]{0:T(512)S(1)} %add_select_fusion.3), kind=kOutput, calls=%fused_computation.6 | convolution fusion | flops 1078329344 | bytes 8395264 | tf_op jit(solution)/shard_map/szxy,yk->szxk/dot_general | solution.py:25
  12.7 0.4 fusion.19
  13.1 1.4 negate_convert_fusion
  14.5 1.4 convolution_convert_fusion
  15.8 0.5 fusion.83
  16.3 0.5 fusion.6
  16.9 1.6 copy.118
  18.4 6.7 %all-to-all-start = ((bf16[4,16,32,256]{3,1,0,2:T(8,128)(2,1)}), bf16[4,16,32,256]{3,1,0,2:T(8,128)(2,1)S(1)}, u32[]{:S(2)}, u32[]{:S(2)}) async-start(bf16[4,16,32,256]{3,1,0,2:T(8,128)(2,1)} %copy.118), calls=%async_computation | async-start | bytes 2097152 | tf_op jit(solution)/shard_map/all_to_all | solution.py:110
  25.1 0.5 fusion.81
  25.6 0.5 fusion.7
  26.1 1.6 copy.120
  27.7 12.6 %all-to-all-done = bf16[4,16,32,256]{3,1,0,2:T(8,128)(2,1)S(1)} async-done(((bf16[4,16,32,256]{3,1,0,2:T(8,128)(2,1)}), bf16[4,16,32,256]{3,1,0,2:T(8,128)(2,1)S(1)}, u32[]{:S(2)}, u32[]{:S(2)}) %all-to-all-start) | async-done | bytes 1048608 | tf_op jit(solution)/shard_map/all_to_all | solution.py:110
  40.2 4.3 %all-to-all-start.1 = ((bf16[4,16,32,256]{3,1,0,2:T(8,128)(2,1)}), bf16[4,16,32,256]{3,1,0,2:T(8,128)(2,1)S(1)}, u32[]{:S(2)}, u32[]{:S(2)}) async-start(bf16[4,16,32,256]{3,1,0,2:T(8,128)(2,1)} %copy.120), calls=%async_computation.1 | async-start | bytes 2097152 | tf_op jit(solution)/shard_map/all_to_all | solution.py:111
  44.6 0.1 copy.119
  44.7 15.0 %all-to-all-done.1 = bf16[4,16,32,256]{3,1,0,2:T(8,128)(2,1)S(1)} async-done(((bf16[4,16,32,256]{3,1,0,2:T(8,128)(2,1)}), bf16[4,16,32,256]{3,1,0,2:T(8,128)(2,1)S(1)}, u32[]{:S(2)}, u32[]{:S(2)}) %all-to-all-start.1) | async-done | bytes 1048608 | tf_op jit(solution)/shard_map/all_to_all | solution.py:111
  59.7 1.0 copy-done
  60.7 1.3 copy.121
  62.0 0.6 fusion.61
  62.6 0.6 subtract_convert_fusion
  63.3 1.8 copy.125
  65.1 10.5 %all-to-all-start.3 = ((bf16[128,4,4,256]{3,2,1,0:T(4,128)(2,1)}), bf16[128,4,4,256]{3,2,1,0:T(4,128)(2,1)S(1)}, u32[]{:S(2)}, u32[]{:S(2)}) async-start(bf16[128,4,4,256]{3,2,1,0:T(4,128)(2,1)} %copy.125), calls=%async_computation.3 | async-start | bytes 2097152 | tf_op jit(solution)/shard_map/all_to_all | solution.py:122
  75.6 0.6 fusion.63
  76.2 0.7 add_convert_fusion
  76.9 1.8 copy.122
  78.7 22.7 %all-to-all-done.3 = bf16[128,4,4,256]{3,2,1,0:T(4,128)(2,1)S(1)} async-done(((bf16[128,4,4,256]{3,2,1,0:T(4,128)(2,1)}), bf16[128,4,4,256]{3,2,1,0:T(4,128)(2,1)S(1)}, u32[]{:S(2)}, u32[]{:S(2)}) %all-to-all-start.3) | async-done | bytes 1048608 | tf_op jit(solution)/shard_map/all_to_all | solution.py:122
  101.4 6.3 %all-to-all-start.2 = ((bf16[128,4,4,256]{3,2,1,0:T(4,128)(2,1)}), bf16[128,4,4,256]{3,2,1,0:T(4,128)(2,1)S(1)}, u32[]{:S(2)}, u32[]{:S(2)}) async-start(bf16[128,4,4,256]{3,2,1,0:T(4,128)(2,1)} %copy.122), calls=%async_computation.2 | async-start | bytes 2097152 | tf_op jit(solution)/shard_map/all_to_all | solution.py:121
  107.7 1.1 gather_fusion.3
  108.8 1.1 gather_fusion.2
  109.9 22.5 %all-to-all-done.2 = bf16[128,4,4,256]{3,2,1,0:T(4,128)(2,1)S(1)} async-done(((bf16[128,4,4,256]{3,2,1,0:T(4,128)(2,1)}), bf16[128,4,4,256]{3,2,1,0:T(4,128)(2,1)S(1)}, u32[]{:S(2)}, u32[]{:S(2)}) %all-to-all-start.2) | async-done | bytes 1048608 | tf_op jit(solution)/shard_map/all_to_all | solution.py:121
  132.4 1.1 gather_fusion.1
  133.5 1.1 gather_fusion
  134.6 1.1 divide_convert_fusion
  135.7 1.2 copy.130
  136.9 7.3 %all-to-all-start.5 = ((bf16[64,4,4,256]{3,2,1,0:T(4,128)(2,1)}), bf16[64,4,4,256]{3,2,1,0:T(4,128)(2,1)S(1)}, u32[]{:S(2)}, u32[]{:S(2)}) async-start(bf16[64,4,4,256]{3,2,1,0:T(4,128)(2,1)} %copy.130), calls=%async_computation.5 | async-start | bytes 1048576 | tf_op jit(solution)/shard_map/all_to_all | solution.py:129
  144.3 1.2 copy.128
  145.5 13.2 %all-to-all-done.5 = bf16[64,4,4,256]{3,2,1,0:T(4,128)(2,1)S(1)} async-done(((bf16[64,4,4,256]{3,2,1,0:T(4,128)(2,1)}), bf16[64,4,4,256]{3,2,1,0:T(4,128)(2,1)S(1)}, u32[]{:S(2)}, u32[]{:S(2)}) %all-to-all-start.5) | async-done | bytes 524320 | tf_op jit(solution)/shard_map/all_to_all | solution.py:129
  158.6 5.9 %all-to-all-start.4 = ((bf16[64,4,4,256]{3,2,1,0:T(4,128)(2,1)}), bf16[64,4,4,256]{3,2,1,0:T(4,128)(2,1)S(1)}, u32[]{:S(2)}, u32[]{:S(2)}) async-start(bf16[64,4,4,256]{3,2,1,0:T(4,128)(2,1)} %copy.128), calls=%async_computation.4 | async-start | bytes 1048576 | tf_op jit(solution)/shard_map/all_to_all | solution.py:128
  164.6 0.2 copy.131
  164.8 0.1 all_to_all.101
  164.9 13.5 %all-to-all-done.4 = bf16[64,4,4,256]{3,2,1,0:T(4,128)(2,1)S(1)} async-done(((bf16[64,4,4,256]{3,2,1,0:T(4,128)(2,1)}), bf16[64,4,4,256]{3,2,1,0:T(4,128)(2,1)S(1)}, u32[]{:S(2)}, u32[]{:S(2)}) %all-to-all-start.4) | async-done | bytes 524320 | tf_op jit(solution)/shard_map/all_to_all | solution.py:128
  178.4 0.2 copy.129
  178.6 0.1 all_to_all.97
  178.7 0.5 fusion.59
  179.2 0.5 fusion.16
  179.8 1.2 copy.132
  181.0 8.6 %all-to-all-start.6 = ((bf16[2,128,4,256]{3,2,0,1:T(4,128)(2,1)}), bf16[2,128,4,256]{3,2,0,1:T(4,128)(2,1)S(1)}, u32[]{:S(2)}, u32[]{:S(2)}) async-start(bf16[2,128,4,256]{3,2,0,1:T(4,128)(2,1)} %copy.132), calls=%async_computation.6 | async-start | bytes 1048576 | tf_op jit(solution)/shard_map/all_to_all | solution.py:133
  189.5 0.5 fusion.57
  190.0 0.5 fusion.15
  190.5 1.2 copy.136
  191.7 7.3 %all-to-all-done.6 = bf16[2,128,4,256]{3,2,0,1:T(4,128)(2,1)S(1)} async-done(((bf16[2,128,4,256]{3,2,0,1:T(4,128)(2,1)}), bf16[2,128,4,256]{3,2,0,1:T(4,128)(2,1)S(1)}, u32[]{:S(2)}, u32[]{:S(2)}) %all-to-all-start.6) | async-done | bytes 524320 | tf_op jit(solution)/shard_map/all_to_all | solution.py:133
  199.0 4.3 %all-to-all-start.7 = ((bf16[2,128,4,256]{3,2,0,1:T(4,128)(2,1)}), bf16[2,128,4,256]{3,2,0,1:T(4,128)(2,1)S(1)}, u32[]{:S(2)}, u32[]{:S(2)}) async-start(bf16[2,128,4,256]{3,2,0,1:T(4,128)(2,1)} %copy.136), calls=%async_computation.7 | async-start | bytes 1048576 | tf_op jit(solution)/shard_map/all_to_all | solution.py:134
  203.3 0.1 copy.133
  203.4 9.3 %all-to-all-done.7 = bf16[2,128,4,256]{3,2,0,1:T(4,128)(2,1)S(1)} async-done(((bf16[2,128,4,256]{3,2,0,1:T(4,128)(2,1)}), bf16[2,128,4,256]{3,2,0,1:T(4,128)(2,1)S(1)}, u32[]{:S(2)}, u32[]{:S(2)}) %all-to-all-start.7) | async-done | bytes 524320 | tf_op jit(solution)/shard_map/all_to_all | solution.py:134
  212.8 0.1 copy.137
  212.9 0.4 fusion.20
  213.3 1.4 fusion.26
  214.7 2.7 %fusion.14 = f32[2,16,32,256]{3,2,1,0:T(8,128)S(1)} fusion(f32[32,2,16,256]{3,0,2,1:T(8,128)} %fusion.26, bf16[2,16,32,256]{3,1,2,0:T(8,128)(2,1)S(1)} %bitcast.132), kind=kOutput, calls=%fused_computation.34 | convolution fusion | flops 152584192 | bytes 2621440 | tf_op jit(solution)/shard_map/pzxk,ky->pzxy/dot_general | solution.py:25
  217.4 2.5 %convolution_subtract_fusion = f32[2,16,32,256]{3,2,1,0:T(8,128)} fusion(f32[2,16,32,256]{3,2,1,0:T(8,128)S(1)} %fusion.14, f32[32,2,16,256]{3,0,2,1:T(8,128)S(1)} %fusion.20, bf16[2,16,32,256]{3,1,2,0:T(8,128)(2,1)S(1)} %bitcast.130), kind=kOutput, calls=%fused_computation.19 | convolution fusion | flops 152846336 | bytes 3670016 | tf_op jit(solution)/shard_map/pzxk,ky->pzxy/dot_general | solution.py:25
  (7 shorter events, 0.1 us)
Async XLA Ops:
  18.4 21.8 %all-to-all-start = ((bf16[4,16,32,256]{3,1,0,2:T(8,128)(2,1)}), bf16[4,16,32,256]{3,1,0,2:T(8,128)(2,1)S(1)}, u32[]{:S(2)}, u32[]{:S(2)}) async-start(bf16[4,16,32,256]{3,1,0,2:T(8,128)(2,1)} %copy.118), calls=%async_computation | async-start | bytes 2097152 | tf_op jit(solution)/shard_map/all_to_all | solution.py:110
  40.2 19.5 %all-to-all-start.1 = ((bf16[4,16,32,256]{3,1,0,2:T(8,128)(2,1)}), bf16[4,16,32,256]{3,1,0,2:T(8,128)(2,1)S(1)}, u32[]{:S(2)}, u32[]{:S(2)}) async-start(bf16[4,16,32,256]{3,1,0,2:T(8,128)(2,1)} %copy.120), calls=%async_computation.1 | async-start | bytes 2097152 | tf_op jit(solution)/shard_map/all_to_all | solution.py:111
  59.7 1.0 copy-start
  65.1 36.3 %all-to-all-start.3 = ((bf16[128,4,4,256]{3,2,1,0:T(4,128)(2,1)}), bf16[128,4,4,256]{3,2,1,0:T(4,128)(2,1)S(1)}, u32[]{:S(2)}, u32[]{:S(2)}) async-start(bf16[128,4,4,256]{3,2,1,0:T(4,128)(2,1)} %copy.125), calls=%async_computation.3 | async-start | bytes 2097152 | tf_op jit(solution)/shard_map/all_to_all | solution.py:122
  101.4 31.0 %all-to-all-start.2 = ((bf16[128,4,4,256]{3,2,1,0:T(4,128)(2,1)}), bf16[128,4,4,256]{3,2,1,0:T(4,128)(2,1)S(1)}, u32[]{:S(2)}, u32[]{:S(2)}) async-start(bf16[128,4,4,256]{3,2,1,0:T(4,128)(2,1)} %copy.122), calls=%async_computation.2 | async-start | bytes 2097152 | tf_op jit(solution)/shard_map/all_to_all | solution.py:121
  136.9 21.7 %all-to-all-start.5 = ((bf16[64,4,4,256]{3,2,1,0:T(4,128)(2,1)}), bf16[64,4,4,256]{3,2,1,0:T(4,128)(2,1)S(1)}, u32[]{:S(2)}, u32[]{:S(2)}) async-start(bf16[64,4,4,256]{3,2,1,0:T(4,128)(2,1)} %copy.130), calls=%async_computation.5 | async-start | bytes 1048576 | tf_op jit(solution)/shard_map/all_to_all | solution.py:129
  158.6 19.8 %all-to-all-start.4 = ((bf16[64,4,4,256]{3,2,1,0:T(4,128)(2,1)}), bf16[64,4,4,256]{3,2,1,0:T(4,128)(2,1)S(1)}, u32[]{:S(2)}, u32[]{:S(2)}) async-start(bf16[64,4,4,256]{3,2,1,0:T(4,128)(2,1)} %copy.128), calls=%async_computation.4 | async-start | bytes 1048576 | tf_op jit(solution)/shard_map/all_to_all | solution.py:128
  181.0 18.1 %all-to-all-start.6 = ((bf16[2,128,4,256]{3,2,0,1:T(4,128)(2,1)}), bf16[2,128,4,256]{3,2,0,1:T(4,128)(2,1)S(1)}, u32[]{:S(2)}, u32[]{:S(2)}) async-start(bf16[2,128,4,256]{3,2,0,1:T(4,128)(2,1)} %copy.132), calls=%async_computation.6 | async-start | bytes 1048576 | tf_op jit(solution)/shard_map/all_to_all | solution.py:133
  199.0 13.8 %all-to-all-start.7 = ((bf16[2,128,4,256]{3,2,0,1:T(4,128)(2,1)}), bf16[2,128,4,256]{3,2,0,1:T(4,128)(2,1)S(1)}, u32[]{:S(2)}, u32[]{:S(2)}) async-start(bf16[2,128,4,256]{3,2,0,1:T(4,128)(2,1)} %copy.136), calls=%async_computation.7 | async-start | bytes 1048576 | tf_op jit(solution)/shard_map/all_to_all | solution.py:134
where the time goes:
time: 221 us; the launch traced here: 220 us
  waiting for transfers between devices  116 us (52%)
  starting transfers between devices  53.9 us (24%)
  local copies, waits for them, and re-layouts  26.5 us (12%)
  matrix products  19.9 us (9%)
  other arithmetic  3.4 us (2%)
    all_to_all x1, waiting for transfers between devices, shards(): lax.all_to_all(out_im, 'tile', split_axis=0, concat_axis=0, tiled=True)  22.7 us
    all_to_all x1, waiting for transfers between devices, shards(): lax.all_to_all(out_re, 'tile', split_axis=0, concat_axis=0, tiled=True)  22.5 us
    dot_general x19, matrix products, product(): return jnp.einsum(form, left, right, preferred_element_type=jnp.float32)  19.9 us
    all_to_all x1, waiting for transfers between devices, shards(): lax.all_to_all(x_im, 'zslab', split_axis=2, concat_axis=1, tiled=True)  15 us
    all_to_all x1, waiting for transfers between devices, shards(): lax.all_to_all(phase_real_part, 'tile', split_axis=0, concat_axis=1, tile...  13.5 us
    all_to_all x1, waiting for transfers between devices, shards(): lax.all_to_all(phase_im, 'tile', split_axis=0, concat_axis=1, tiled=True)  13.2 us
    all_to_all x1, waiting for transfers between devices, shards(): lax.all_to_all(x_re, 'zslab', split_axis=2, concat_axis=1, tiled=True)  12.6 us
    all_to_all x1, starting transfers between devices, shards(): lax.all_to_all(out_im, 'tile', split_axis=0, concat_axis=0, tiled=True)  10.5 us
  transfers between devices with their start and end apart: 8, of which 8 were waited for; matrix products, arithmetic and copies ran while one was open for 5% of the time, Pallas kernels for 0%

commit v1 on v0

--- a/solution.py
+++ b/solution.py
@@ -1,3 +1,4 @@
+import functools
 import math
 import jax
 import jax.numpy as jnp
@@ -8,6 +9,34 @@
 GY = 256
 GZ = 128
 FACES = 4
+
+
+def trees_fill(values, array_dim, local_array):
+    now, extra = (values.shape[:array_dim], values.shape[array_dim + 1 :])
+    return jnp.moveaxis(values.reshape(*now, local_array, -1, *extra), array_dim, 0)
+
+
+def review_units(slab_in, in_dim):
+    upper = list(slab_in.shape[1:])
+    upper[in_dim] *= slab_in.shape[0]
+    return jnp.moveaxis(slab_in, 0, in_dim).reshape(upper)
+
+
+def _group_things(block_here, dev_axis, x0, original):
+    kept_arr, formed = (jax.lax.axis_size(dev_axis), jax.lax.axis_index(dev_axis))
+    f_now = trees_fill(block_here, x0, kept_arr)
+    fresh = f_now
+    for ii in [*range(1, kept_arr)]:
+        h_now, r1 = ((formed + ii) % kept_arr, (formed - ii) % kept_arr)
+        r_now = lax.dynamic_index_in_dim(f_now, h_now, 0)
+        big = jax.lax.ppermute(
+            r_now, dev_axis, perm=[(num, (num + ii) % kept_arr) for num in range(kept_arr)]
+        )
+        fresh = lax.dynamic_update_slice_in_dim(fresh, big, r1, axis=0)
+    return review_units(fresh, original)
+
+
+get_plate = functools.partial(_group_things, dev_axis="zslab", x0=1, original=2)
 
 
 def dft_tables(length):
@@ -131,7 +160,7 @@
     w_re, w_im = inverse_z(returned[0], returned[1], tables_z)
     v_re, v_im = inverse_x(
         lax.all_to_all(w_re, "zslab", split_axis=1, concat_axis=2, tiled=True),
-        lax.all_to_all(w_im, "zslab", split_axis=1, concat_axis=2, tiled=True),
+        get_plate(w_im),
         tables_x,
     )
     return product("pzxk,ky->pzxy", v_re, tables_y[0]) - product("pzxk,ky->pzxy", v_im, tables_y[1])

time: 221 us -> 213 us (0.964)
  waiting for transfers between devices: 116 us -> 104 us
  starting transfers between devices: 53.9 us -> 58.6 us
    ppermute x0 -> x7, starting transfers between devices: none -> 14.1 us  [_group_things(): jax.lax.ppermute(r_now, dev_axis, perm=[(num, (num + ii) % kept_arr) for...]
    all_to_all x1 -> x0, waiting for transfers between devices: 9.34 us -> none  [shards(): lax.all_to_all(w_im, 'zslab', split_axis=1, concat_axis=2, tiled=True)]
    all_to_all x1, waiting for transfers between devices: 7.29 us -> 0.01 us  [shards(): lax.all_to_all(w_re, 'zslab', split_axis=1, concat_axis=2, tiled=True)]
    ppermute x0 -> x7, waiting for transfers between devices: none -> 6.91 us  [_group_things(): jax.lax.ppermute(r_now, dev_axis, perm=[(num, (num + ii) % kept_arr) for...]
    all_to_all x1, starting transfers between devices: 8.56 us -> 3.44 us  [shards(): lax.all_to_all(w_re, 'zslab', split_axis=1, concat_axis=2, tiled=True)]
    all_to_all x1 -> x0, starting transfers between devices: 4.27 us -> none  [shards(): lax.all_to_all(w_im, 'zslab', split_axis=1, concat_axis=2, tiled=True)]
    all_to_all x1, starting transfers between devices: 10.5 us -> 6.34 us  [shards(): lax.all_to_all(out_im, 'tile', split_axis=0, concat_axis=0, tiled=True)]
    all_to_all x1, starting transfers between devices: 6.34 us -> 10.5 us  [shards(): lax.all_to_all(out_re, 'tile', split_axis=0, concat_axis=0, tiled=True)]
  transfers between devices with their start and end apart: 8 -> 14, of which waited for: 8 -> 8; matrix products, arithmetic and copies ran while one was open for 5% -> 6% of each run, Pallas kernels for 0% -> 0%
where the time goes in v1:
time: 213 us; the launch traced here: 212 us
  waiting for transfers between devices  104 us (49%)
  starting transfers between devices  58.6 us (28%)
  local copies, waits for them, and re-layouts  24.6 us (12%)
  matrix products  21.3 us (10%)
  other arithmetic  3.4 us (2%)
    all_to_all x1, waiting for transfers between devices, shards(): lax.all_to_all(out_re, 'tile', split_axis=0, concat_axis=0, tiled=True)  22.7 us
    all_to_all x1, waiting for transfers between devices, shards(): lax.all_to_all(out_im, 'tile', split_axis=0, concat_axis=0, tiled=True)  22.5 us
    dot_general x19, matrix products, product(): return jnp.einsum(form, left, right, preferred_element_type=jnp.float32)  21.3 us
    ppermute x7, starting transfers between devices, _group_things(): jax.lax.ppermute(r_now, dev_axis, perm=[(num, (num + ii) % kept_arr) for...  14.1 us
    all_to_all x1, waiting for transfers between devices, shards(): lax.all_to_all(phase_im, 'tile', split_axis=0, concat_axis=1, tiled=True)  13.2 us
    all_to_all x1, waiting for transfers between devices, shards(): lax.all_to_all(x_im, 'zslab', split_axis=2, concat_axis=1, tiled=True)  13 us
    all_to_all x1, waiting for transfers between devices, shards(): lax.all_to_all(phase_real_part, 'tile', split_axis=0, concat_axis=1, tile...  12.7 us
    all_to_all x1, waiting for transfers between devices, shards(): lax.all_to_all(x_re, 'zslab', split_axis=2, concat_axis=1, tiled=True)  12.5 us
  transfers between devices with their start and end apart: 14, of which 8 were waited for; matrix products, arithmetic and copies ran while one was open for 6% of the time, Pallas kernels for 0%

profile of v1, /device:TPU:1, one launch (start us, length us, event | category | flops | bytes accessed | tf_op | source)
XLA Modules:
  0.0 212.0 jit_solution(9550794647022363964)
XLA Ops:
  0.0 0.8 fusion.119
  0.9 0.8 multiply_reduce_fusion
  1.8 7.2 %reshape.198 = bf16[4,16,32,2,512]{4,3,2,1,0:T(2,128)(2,1)} reshape(bf16[1,4,16,64,512]{4,3,2,1,0:T(8,128)(2,1)} %param.3) | data formatting | bytes 8388608 | tf_op jit(solution)/shard_map/reshape | solution.py:128
  9.1 3.6 %fusion.1 = f32[4,16,32,2,256]{4,2,3,1,0:T(8,128)S(1)} fusion(bf16[4,16,32,2,512]{4,3,2,1,0:T(2,128)(2,1)} %reshape.198, bf16[4,512]{1,0:T(4,128)(2,1)S(1)} %fusion.84, bf16[4,32,2]{1,2,0:T(2,128)(2,1)S(1)} %compare_convert_fusion, s32[512]{0:T(512)S(1)} %add_select_fusion.3), kind=kOutput, calls=%fused_computation.6 | convolution fusion | flops 1078329344 | bytes 8395264 | tf_op jit(solution)/shard_map/szxy,yk->szxk/dot_general | solution.py:54
  12.7 0.4 fusion.18
  13.0 1.4 convolution_convert_fusion
  14.4 1.4 negate_convert_fusion
  15.8 0.5 fusion.82
  16.3 0.5 fusion.6
  16.8 1.6 copy.110
  18.4 6.7 %all-to-all-start = ((bf16[4,16,32,256]{3,1,0,2:T(8,128)(2,1)}), bf16[4,16,32,256]{3,1,0,2:T(8,128)(2,1)S(1)}, u32[]{:S(2)}, u32[]{:S(2)}) async-start(bf16[4,16,32,256]{3,1,0,2:T(8,128)(2,1)} %copy.110), calls=%async_computation | async-start | bytes 2097152 | tf_op jit(solution)/shard_map/all_to_all | solution.py:139
  25.1 0.5 fusion.80
  25.6 0.5 fusion.7
  26.1 1.6 copy.112
  27.7 12.5 %all-to-all-done = bf16[4,16,32,256]{3,1,0,2:T(8,128)(2,1)S(1)} async-done(((bf16[4,16,32,256]{3,1,0,2:T(8,128)(2,1)}), bf16[4,16,32,256]{3,1,0,2:T(8,128)(2,1)S(1)}, u32[]{:S(2)}, u32[]{:S(2)}) %all-to-all-start) | async-done | bytes 1048608 | tf_op jit(solution)/shard_map/all_to_all | solution.py:139
  40.2 4.3 %all-to-all-start.1 = ((bf16[4,16,32,256]{3,1,0,2:T(8,128)(2,1)}), bf16[4,16,32,256]{3,1,0,2:T(8,128)(2,1)S(1)}, u32[]{:S(2)}, u32[]{:S(2)}) async-start(bf16[4,16,32,256]{3,1,0,2:T(8,128)(2,1)} %copy.112), calls=%async_computation.1 | async-start | bytes 2097152 | tf_op jit(solution)/shard_map/all_to_all | solution.py:140
  44.6 0.1 copy.111
  44.7 2.0 fusion.62
  46.6 13.0 %all-to-all-done.1 = bf16[4,16,32,256]{3,1,0,2:T(8,128)(2,1)S(1)} async-done(((bf16[4,16,32,256]{3,1,0,2:T(8,128)(2,1)}), bf16[4,16,32,256]{3,1,0,2:T(8,128)(2,1)S(1)}, u32[]{:S(2)}, u32[]{:S(2)}) %all-to-all-start.1) | async-done | bytes 1048608 | tf_op jit(solution)/shard_map/all_to_all | solution.py:140
  59.7 0.1 copy.113
  59.8 1.5 copy-done
  61.3 0.6 add_convert_fusion
  61.9 1.8 copy.114
  63.7 10.5 %all-to-all-start.2 = ((bf16[128,4,4,256]{3,2,1,0:T(4,128)(2,1)}), bf16[128,4,4,256]{3,2,1,0:T(4,128)(2,1)S(1)}, u32[]{:S(2)}, u32[]{:S(2)}) async-start(bf16[128,4,4,256]{3,2,1,0:T(4,128)(2,1)} %copy.114), calls=%async_computation.2 | async-start | bytes 2097152 | tf_op jit(solution)/shard_map/all_to_all | solution.py:150
  74.2 0.6 fusion.60
  74.9 0.7 subtract_convert_fusion
  75.5 1.8 copy.117
  77.3 22.7 %all-to-all-done.2 = bf16[128,4,4,256]{3,2,1,0:T(4,128)(2,1)S(1)} async-done(((bf16[128,4,4,256]{3,2,1,0:T(4,128)(2,1)}), bf16[128,4,4,256]{3,2,1,0:T(4,128)(2,1)S(1)}, u32[]{:S(2)}, u32[]{:S(2)}) %all-to-all-start.2) | async-done | bytes 1048608 | tf_op jit(solution)/shard_map/all_to_all | solution.py:150
  100.0 6.3 %all-to-all-start.3 = ((bf16[128,4,4,256]{3,2,1,0:T(4,128)(2,1)}), bf16[128,4,4,256]{3,2,1,0:T(4,128)(2,1)S(1)}, u32[]{:S(2)}, u32[]{:S(2)}) async-start(bf16[128,4,4,256]{3,2,1,0:T(4,128)(2,1)} %copy.117), calls=%async_computation.3 | async-start | bytes 2097152 | tf_op jit(solution)/shard_map/all_to_all | solution.py:151
  106.3 1.1 gather_fusion.1
  107.5 1.1 gather_fusion
  108.6 22.5 %all-to-all-done.3 = bf16[128,4,4,256]{3,2,1,0:T(4,128)(2,1)S(1)} async-done(((bf16[128,4,4,256]{3,2,1,0:T(4,128)(2,1)}), bf16[128,4,4,256]{3,2,1,0:T(4,128)(2,1)S(1)}, u32[]{:S(2)}, u32[]{:S(2)}) %all-to-all-start.3) | async-done | bytes 1048608 | tf_op jit(solution)/shard_map/all_to_all | solution.py:151
  131.0 1.1 gather_fusion.2
  132.1 1.1 gather_fusion.3
  133.2 1.1 divide_convert_fusion
  134.4 1.2 copy.122
  135.6 7.3 %all-to-all-start.5 = ((bf16[64,4,4,256]{3,2,1,0:T(4,128)(2,1)}), bf16[64,4,4,256]{3,2,1,0:T(4,128)(2,1)S(1)}, u32[]{:S(2)}, u32[]{:S(2)}) async-start(bf16[64,4,4,256]{3,2,1,0:T(4,128)(2,1)} %copy.122), calls=%async_computation.5 | async-start | bytes 1048576 | tf_op jit(solution)/shard_map/all_to_all | solution.py:158
  142.9 1.2 copy.120
  144.1 13.2 %all-to-all-done.5 = bf16[64,4,4,256]{3,2,1,0:T(4,128)(2,1)S(1)} async-done(((bf16[64,4,4,256]{3,2,1,0:T(4,128)(2,1)}), bf16[64,4,4,256]{3,2,1,0:T(4,128)(2,1)S(1)}, u32[]{:S(2)}, u32[]{:S(2)}) %all-to-all-start.5) | async-done | bytes 524320 | tf_op jit(solution)/shard_map/all_to_all | solution.py:158
  157.3 5.9 %all-to-all-start.4 = ((bf16[64,4,4,256]{3,2,1,0:T(4,128)(2,1)}), bf16[64,4,4,256]{3,2,1,0:T(4,128)(2,1)S(1)}, u32[]{:S(2)}, u32[]{:S(2)}) async-start(bf16[64,4,4,256]{3,2,1,0:T(4,128)(2,1)} %copy.120), calls=%async_computation.4 | async-start | bytes 1048576 | tf_op jit(solution)/shard_map/all_to_all | solution.py:157
  163.5 0.2 copy.123
  163.7 0.1 all_to_all.88
  163.8 0.5 fusion.56
  164.3 12.7 %all-to-all-done.4 = bf16[64,4,4,256]{3,2,1,0:T(4,128)(2,1)S(1)} async-done(((bf16[64,4,4,256]{3,2,1,0:T(4,128)(2,1)}), bf16[64,4,4,256]{3,2,1,0:T(4,128)(2,1)S(1)}, u32[]{:S(2)}, u32[]{:S(2)}) %all-to-all-start.4) | async-done | bytes 524320 | tf_op jit(solution)/shard_map/all_to_all | solution.py:157
  177.1 0.2 copy.121
  177.3 0.1 all_to_all.84
  177.4 0.5 fusion.58
  177.9 0.5 fusion.9
  178.5 5.4 %collective-permute-start = (bf16[1,2,16,4,256]{4,2,3,0,1:T(8,128)(2,1)S(1)}, bf16[1,2,16,4,256]{4,2,3,0,1:T(8,128)(2,1)S(1)}, u32[]{:S(2)}, u32[]{:S(2)}) collective-permute-start(bf16[1,2,16,4,256]{4,2,3,0,1:T(8,128)(2,1)S(1)} %get-tuple-element.13), channel_id=1, source_target_pairs={{0,1},{1,2},{2,3},{3,4},{4,5},{5,6},{6,7},{7,0},{8,9},{9,10},{10,1... | collective-permute-start | bytes 196616 | tf_op jit(solution)/shard_map/ppermute | solution.py:32
  183.9 1.1 collective-permute-start.1
  185.0 1.0 collective-permute-start.2
  186.0 1.4 collective-permute-start.3
  187.5 2.6 %collective-permute-start.4 = (bf16[1,2,16,4,256]{4,2,3,0,1:T(8,128)(2,1)S(1)}, bf16[1,2,16,4,256]{4,2,3,0,1:T(8,128)(2,1)S(1)}, u32[]{:S(2)}, u32[]{:S(2)}) collective-permute-start(bf16[1,2,16,4,256]{4,2,3,0,1:T(8,128)(2,1)S(1)} %get-tuple-element.9), channel_id=1, source_target_pairs={{0,5},{1,6},{2,7},{3,0},{4,1},{5,2},{6,3},{7,4},{8,13},{9,14},{10,... | collective-permute-start | bytes 196616 | tf_op jit(solution)/shard_map/ppermute | solution.py:32
  190.1 0.5 fusion.15
  190.6 1.2 copy.124
  191.8 3.4 %all-to-all-start.6 = ((bf16[2,128,4,256]{3,2,0,1:T(4,128)(2,1)}), bf16[2,128,4,256]{3,2,0,1:T(4,128)(2,1)S(1)}, u32[]{:S(2)}, u32[]{:S(2)}) async-start(bf16[2,128,4,256]{3,2,0,1:T(4,128)(2,1)} %copy.124), calls=%async_computation.6 | async-start | bytes 1048576 | tf_op jit(solution)/shard_map/all_to_all | solution.py:162
  195.3 1.9 collective-permute-start.5
  197.1 0.7 collective-permute-start.6
  197.9 6.0 %collective-permute-done.5 = bf16[1,2,16,4,256]{4,2,3,0,1:T(8,128)(2,1)S(1)} collective-permute-done((bf16[1,2,16,4,256]{4,2,3,0,1:T(8,128)(2,1)S(1)}, bf16[1,2,16,4,256]{4,2,3,0,1:T(8,128)(2,1)S(1)}, u32[]{:S(2)}, u32[]{:S(2)}) %collective-permute-start.5) | collective-permute-done | bytes 65568 | tf_op jit(solution)/shard_map/ppermute | solution.py:32
  203.9 0.9 collective-permute-done.6
  205.0 1.4 fusion.25
  206.4 0.4 fusion.23
  206.7 2.7 %fusion.14 = f32[2,16,32,256]{3,2,1,0:T(8,128)S(1)} fusion(f32[32,2,16,256]{3,0,2,1:T(8,128)} %fusion.25, bf16[2,16,32,256]{3,1,2,0:T(8,128)(2,1)S(1)} %bitcast.147), kind=kOutput, calls=%fused_computation.34 | convolution fusion | flops 152584192 | bytes 2621440 | tf_op jit(solution)/shard_map/pzxk,ky->pzxy/dot_general | solution.py:54
  209.5 2.5 %convolution_subtract_fusion = f32[2,16,32,256]{3,2,1,0:T(8,128)} fusion(f32[2,16,32,256]{3,2,1,0:T(8,128)S(1)} %fusion.14, f32[32,2,16,256]{3,0,2,1:T(8,128)S(1)} %fusion.23, bf16[2,16,32,256]{3,1,2,0:T(8,128)(2,1)S(1)} %bitcast.148), kind=kOutput, calls=%fused_computation.19 | convolution fusion | flops 152846336 | bytes 3670016 | tf_op jit(solution)/shard_map/pzxk,ky->pzxy/dot_general | solution.py:54
  (25 shorter events, 0.6 us)
Async XLA Ops:
  18.4 21.8 %all-to-all-start = ((bf16[4,16,32,256]{3,1,0,2:T(8,128)(2,1)}), bf16[4,16,32,256]{3,1,0,2:T(8,128)(2,1)S(1)}, u32[]{:S(2)}, u32[]{:S(2)}) async-start(bf16[4,16,32,256]{3,1,0,2:T(8,128)(2,1)} %copy.110), calls=%async_computation | async-start | bytes 2097152 | tf_op jit(solution)/shard_map/all_to_all | solution.py:139
  40.2 19.5 %all-to-all-start.1 = ((bf16[4,16,32,256]{3,1,0,2:T(8,128)(2,1)}), bf16[4,16,32,256]{3,1,0,2:T(8,128)(2,1)S(1)}, u32[]{:S(2)}, u32[]{:S(2)}) async-start(bf16[4,16,32,256]{3,1,0,2:T(8,128)(2,1)} %copy.112), calls=%async_computation.1 | async-start | bytes 2097152 | tf_op jit(solution)/shard_map/all_to_all | solution.py:140
  59.7 1.6 copy-start
  63.7 36.3 %all-to-all-start.2 = ((bf16[128,4,4,256]{3,2,1,0:T(4,128)(2,1)}), bf16[128,4,4,256]{3,2,1,0:T(4,128)(2,1)S(1)}, u32[]{:S(2)}, u32[]{:S(2)}) async-start(bf16[128,4,4,256]{3,2,1,0:T(4,128)(2,1)} %copy.114), calls=%async_computation.2 | async-start | bytes 2097152 | tf_op jit(solution)/shard_map/all_to_all | solution.py:150
  100.0 31.0 %all-to-all-start.3 = ((bf16[128,4,4,256]{3,2,1,0:T(4,128)(2,1)}), bf16[128,4,4,256]{3,2,1,0:T(4,128)(2,1)S(1)}, u32[]{:S(2)}, u32[]{:S(2)}) async-start(bf16[128,4,4,256]{3,2,1,0:T(4,128)(2,1)} %copy.117), calls=%async_computation.3 | async-start | bytes 2097152 | tf_op jit(solution)/shard_map/all_to_all | solution.py:151
  135.6 21.7 %all-to-all-start.5 = ((bf16[64,4,4,256]{3,2,1,0:T(4,128)(2,1)}), bf16[64,4,4,256]{3,2,1,0:T(4,128)(2,1)S(1)}, u32[]{:S(2)}, u32[]{:S(2)}) async-start(bf16[64,4,4,256]{3,2,1,0:T(4,128)(2,1)} %copy.122), calls=%async_computation.5 | async-start | bytes 1048576 | tf_op jit(solution)/shard_map/all_to_all | solution.py:158
  157.3 19.8 %all-to-all-start.4 = ((bf16[64,4,4,256]{3,2,1,0:T(4,128)(2,1)}), bf16[64,4,4,256]{3,2,1,0:T(4,128)(2,1)S(1)}, u32[]{:S(2)}, u32[]{:S(2)}) async-start(bf16[64,4,4,256]{3,2,1,0:T(4,128)(2,1)} %copy.120), calls=%async_computation.4 | async-start | bytes 1048576 | tf_op jit(solution)/shard_map/all_to_all | solution.py:157
  178.5 16.7 %collective-permute-start = (bf16[1,2,16,4,256]{4,2,3,0,1:T(8,128)(2,1)S(1)}, bf16[1,2,16,4,256]{4,2,3,0,1:T(8,128)(2,1)S(1)}, u32[]{:S(2)}, u32[]{:S(2)}) collective-permute-start(bf16[1,2,16,4,256]{4,2,3,0,1:T(8,128)(2,1)S(1)} %get-tuple-element.13), channel_id=1, source_target_pairs={{0,1},{1,2},{2,3},{3,4},{4,5},{5,6},{6,7},{7,0},{8,9},{9,10},{10,1... | collective-permute-start | bytes 196616 | tf_op jit(solution)/shard_map/ppermute | solution.py:32
  183.9 13.3 %collective-permute-start.1 = (bf16[1,2,16,4,256]{4,2,3,0,1:T(8,128)(2,1)S(1)}, bf16[1,2,16,4,256]{4,2,3,0,1:T(8,128)(2,1)S(1)}, u32[]{:S(2)}, u32[]{:S(2)}) collective-permute-start(bf16[1,2,16,4,256]{4,2,3,0,1:T(8,128)(2,1)S(1)} %get-tuple-element.12), channel_id=1, source_target_pairs={{0,2},{1,3},{2,4},{3,5},{4,6},{5,7},{6,0},{7,1},{8,10},{9,11},{10,... | collective-permute-start | bytes 196616 | tf_op jit(solution)/shard_map/ppermute | solution.py:32
  185.0 12.8 %collective-permute-start.2 = (bf16[1,2,16,4,256]{4,2,3,0,1:T(8,128)(2,1)S(1)}, bf16[1,2,16,4,256]{4,2,3,0,1:T(8,128)(2,1)S(1)}, u32[]{:S(2)}, u32[]{:S(2)}) collective-permute-start(bf16[1,2,16,4,256]{4,2,3,0,1:T(8,128)(2,1)S(1)} %get-tuple-element.11), channel_id=1, source_target_pairs={{0,3},{1,4},{2,5},{3,6},{4,7},{5,0},{6,1},{7,2},{8,11},{9,12},{10,... | collective-permute-start | bytes 196616 | tf_op jit(solution)/shard_map/ppermute | solution.py:32
  186.0 11.8 %collective-permute-start.3 = (bf16[1,2,16,4,256]{4,2,3,0,1:T(8,128)(2,1)S(1)}, bf16[1,2,16,4,256]{4,2,3,0,1:T(8,128)(2,1)S(1)}, u32[]{:S(2)}, u32[]{:S(2)}) collective-permute-start(bf16[1,2,16,4,256]{4,2,3,0,1:T(8,128)(2,1)S(1)} %get-tuple-element.10), channel_id=1, source_target_pairs={{0,4},{1,5},{2,6},{3,7},{4,0},{5,1},{6,2},{7,3},{8,12},{9,13},{10,... | collective-permute-start | bytes 196616 | tf_op jit(solution)/shard_map/ppermute | solution.py:32
  187.5 10.4 %collective-permute-start.4 = (bf16[1,2,16,4,256]{4,2,3,0,1:T(8,128)(2,1)S(1)}, bf16[1,2,16,4,256]{4,2,3,0,1:T(8,128)(2,1)S(1)}, u32[]{:S(2)}, u32[]{:S(2)}) collective-permute-start(bf16[1,2,16,4,256]{4,2,3,0,1:T(8,128)(2,1)S(1)} %get-tuple-element.9), channel_id=1, source_target_pairs={{0,5},{1,6},{2,7},{3,0},{4,1},{5,2},{6,3},{7,4},{8,13},{9,14},{10,... | collective-permute-start | bytes 196616 | tf_op jit(solution)/shard_map/ppermute | solution.py:32
  191.8 13.0 %all-to-all-start.6 = ((bf16[2,128,4,256]{3,2,0,1:T(4,128)(2,1)}), bf16[2,128,4,256]{3,2,0,1:T(4,128)(2,1)S(1)}, u32[]{:S(2)}, u32[]{:S(2)}) async-start(bf16[2,128,4,256]{3,2,0,1:T(4,128)(2,1)} %copy.124), calls=%async_computation.6 | async-start | bytes 1048576 | tf_op jit(solution)/shard_map/all_to_all | solution.py:162
  195.3 8.7 %collective-permute-start.5 = (bf16[1,2,16,4,256]{4,2,3,0,1:T(8,128)(2,1)S(1)}, bf16[1,2,16,4,256]{4,2,3,0,1:T(8,128)(2,1)S(1)}, u32[]{:S(2)}, u32[]{:S(2)}) collective-permute-start(bf16[1,2,16,4,256]{4,2,3,0,1:T(8,128)(2,1)S(1)} %get-tuple-element.8), channel_id=1, source_target_pairs={{0,6},{1,7},{2,0},{3,1},{4,2},{5,3},{6,4},{7,5},{8,14},{9,15},{10,... | collective-permute-start | bytes 196616 | tf_op jit(solution)/shard_map/ppermute | solution.py:32
  197.1 7.7 %collective-permute-start.6 = (bf16[1,2,16,4,256]{4,2,3,0,1:T(8,128)(2,1)S(1)}, bf16[1,2,16,4,256]{4,2,3,0,1:T(8,128)(2,1)S(1)}, u32[]{:S(2)}, u32[]{:S(2)}) collective-permute-start(bf16[1,2,16,4,256]{4,2,3,0,1:T(8,128)(2,1)S(1)} %get-tuple-element.7), channel_id=1, source_target_pairs={{0,7},{1,0},{2,1},{3,2},{4,3},{5,4},{6,5},{7,6},{8,15},{9,8},{10,9... | collective-permute-start | bytes 196616 | tf_op jit(solution)/shard_map/ppermute | solution.py:32
